TPU v7x, 32 devices: a whole 2x2x4 slice. The times are simulated.
32 devices in a mesh: sec: 2 (over core), horiz: 4 (over z), lev: 4 (over y, x).
Axes of the slice: x: 2, y: 2, z: 4, core: 2. Of those that a mesh axis runs over, the one named last changes fastest.
Arguments:
- state: float32 [2, 80, 384, 128], P('sec', 'lev', 'horiz'), may hold values from -6 to 6
- diffusivity: float32 [2, 384, 128], P('sec', 'horiz'), may hold values from 0.02 to 0.24
- coupling_mask: int32 [2, 384, 128], P('sec', ('horiz', 'lev')), may hold values 0 or 1
- pair_rows: int32 [2, 384, 3], P('sec', ('horiz', 'lev')), may hold values from 0 to 383, as said below
- pair_counts: int32 [2, 384], P('sec', ('horiz', 'lev')), may hold values from 1 to 3
- remap_weights: bfloat16 [2, 384, 3, 128, 128], P('sec', ('horiz', 'lev')), may hold values from -0.3125 to 0.3125
- export_profile: float32 [2, 80], P('sec'), may hold values from 0.02 to 0.3
- import_profile: float32 [2, 80], P('sec'), may hold values from 0.1 to 1
- column_inverse: float32 [2, 80, 80], P('sec'), may hold values from -1 to 2
Outputs:
- new_state: float32 [2, 80, 384, 128], P('sec', 'lev', 'horiz')
- forcing: float32 [2, 384, 128], P('sec', ('horiz', 'lev'))
Inputs may be any that keep to these rules, and one draw needn't show every extreme that they name: `pair_rows`: rows are grouped in aligned blocks of 24; for a row whose block starts at b, each entry p satisfies (p - b + 8) mod 384 < 40. Entries at positions of at least the row's count are padding.
All inputs are finite; a program needn't handle non-finite values. No bound on the sum of `coupling_mask` on one device may be relied on, other than what follows from the above.
Results may differ from a plain program's by a relative error of at most 0.0029.
Values may be sent and summed in bfloat16 or wider, within the bound.
A program may use at most 64 MiB of HBM per device.

v0:
```python
import jax
import jax.numpy as jnp
from jax import lax
from jax.sharding import PartitionSpec as P

REACH = 8
ATM_STEPS = 4
OCN_STEPS = 2


def padded(cells, sides, width):
    for axis, dim in sides:
        count = lax.axis_size(axis)
        head = lax.slice_in_dim(cells, 0, width, axis=dim)
        tail = lax.slice_in_dim(cells, cells.shape[dim] - width, cells.shape[dim], axis=dim)
        cells = jnp.concatenate(
            [
                lax.ppermute(tail, axis, [(i, (i + 1) % count) for i in range(count)]),
                cells,
                lax.ppermute(head, axis, [((i + 1) % count, i) for i in range(count)]),
            ],
            axis=dim,
        )
    return cells


def partner_2(block, axis, bit):
    count = lax.axis_size(axis)
    route = []
    for low in range(count):
        high = low | 1 << bit
        if high != low and high < count:
            route += [(low, high), (high, low)]
    return lax.ppermute(block, axis, route)


def per_device(
    state,
    diffusivity,
    coupling_mask,
    pair_rows,
    pair_counts,
    remap_weights,
    export_profile,
    import_profile,
    column_inverse,
):
    current = state[0]
    kappa = diffusivity[0]
    section = lax.axis_index("sec")
    steps_here = jnp.where(section == 0, ATM_STEPS, OCN_STEPS)
    level_count = current.shape[0]
    stacked = jnp.concatenate([current, kappa[None]], axis=0)
    extended = padded(stacked, (("horiz", 1),), ATM_STEPS)
    values = extended[:level_count]
    kappa_wide = extended[level_count]
    for step_index in range(ATM_STEPS):
        middle = values[:, 1:-1]
        kappa_mid = kappa_wide[step_index + 1 : kappa_wide.shape[0] - step_index - 1]
        stencil = (
            values[:, :-2]
            + values[:, 2:]
            + jnp.roll(middle, 1, 2)
            + jnp.roll(middle, -1, 2)
            - 4.0 * middle
        )
        values = jnp.where(step_index < steps_here, middle + kappa_mid[None] * stencil, middle)
    current = values
    columns = lax.all_to_all(current, "lev", split_axis=1, concat_axis=0, tiled=True)
    surface_out = jnp.tensordot(
        export_profile[0], columns, axes=(0, 0), precision=lax.Precision.HIGHEST
    ).astype(jnp.bfloat16)
    partner = partner_2(surface_out, "sec", 0)
    block_count = partner.shape[0]
    first_row = lax.axis_index(("horiz", "lev")) * block_count
    rows_total = block_count * lax.axis_size(("horiz", "lev"))
    source_ids = pair_rows[0]
    window = padded(partner, ((("horiz", "lev"), 0),), REACH)
    local_rows = jnp.mod(source_ids - first_row + REACH, rows_total)
    sources = window[local_rows]
    usable = lax.broadcasted_iota(jnp.int32, source_ids.shape, 1) < pair_counts[0][:, None]
    sources = jnp.where(usable[:, :, None], sources, jnp.zeros((), sources.dtype))
    forcing = jnp.einsum(
        "rkw,rkwv->rv", sources, remap_weights[0], preferred_element_type=jnp.float32
    )
    masked = forcing * coupling_mask[0].astype(jnp.float32)
    columns = columns + import_profile[0][:, None, None] * masked[None]
    level_total, row_count, cell_count = columns.shape
    flat_columns = columns.reshape(level_total, row_count * cell_count)
    mixed_columns = jnp.dot(
        column_inverse[0],
        flat_columns,
        precision=lax.Precision.HIGHEST,
        preferred_element_type=jnp.float32,
    )
    mixed_columns = mixed_columns.reshape(level_total, row_count, cell_count)
    new_state = lax.all_to_all(mixed_columns, "lev", split_axis=0, concat_axis=1, tiled=True)
    return (new_state[None], forcing[None])


def solution(mesh):
    placed = (
        P("sec", "lev", "horiz", None),
        P("sec", "horiz", None),
        P("sec", ("horiz", "lev"), None),
        P("sec", ("horiz", "lev"), None),
        P("sec", ("horiz", "lev")),
        P("sec", ("horiz", "lev"), None, None, None),
        P("sec", None),
        P("sec", None),
        P("sec", None, None),
    )
    return jax.shard_map(
        per_device,
        mesh=mesh,
        in_specs=placed,
        out_specs=(P("sec", "lev", "horiz", None), P("sec", ("horiz", "lev"), None)),
        check_vma=False,
    )
```

profile of v0, /device:TPU:0, one launch (start us, length us, event | category | flops | bytes accessed | tf_op | source)
XLA Modules:
  0.0 79.2 jit_solution(13026328614662269850)
XLA Ops:
  0.6 0.0 copy-start
  0.6 0.0 copy-start.2
  0.7 1.9 %copy.51 = f32[1,20,96,128]{3,1,2,0:T(8,128)S(1)} copy(f32[1,20,96,128]{3,2,1,0:T(8,128)} %param.9) | data formatting | bytes 1966080 | tf_op args[0]
  2.6 0.0 copy-done.2
  2.6 0.7 pad_maximum_fusion.5
  3.3 3.0 %collective-permute-start = (f32[21,4,128]{2,0,1:T(8,128)}, f32[21,4,128]{2,0,1:T(8,128)}, u32[]{:S(2)}, u32[]{:S(2)}) collective-permute-start(f32[21,4,128]{2,0,1:T(8,128)} %get-tuple-element.14), channel_id=1, source_target_pairs={{0,4},{4,8},{8,12},{12,0},{1,5},{5,9},{9,13},{13,1},{2,6},{6,10},{... | collective-permute-start | bytes 129032 | tf_op jit(solution)/shard_map/ppermute | solution.py:18
  6.3 2.0 %collective-permute-start.1 = (f32[21,4,128]{2,0,1:T(8,128)}, f32[21,4,128]{2,0,1:T(8,128)}, u32[]{:S(2)}, u32[]{:S(2)}) collective-permute-start(f32[21,4,128]{2,0,1:T(8,128)} %get-tuple-element.15), channel_id=1, source_target_pairs={{4,0},{8,4},{12,8},{0,12},{5,1},{9,5},{13,9},{1,13},{6,2},{10,6},{... | collective-permute-start | bytes 129032 | tf_op jit(solution)/shard_map/ppermute | solution.py:20
  8.3 2.5 %collective-permute-done = f32[21,4,128]{2,0,1:T(8,128)} collective-permute-done((f32[21,4,128]{2,0,1:T(8,128)}, f32[21,4,128]{2,0,1:T(8,128)}, u32[]{:S(2)}, u32[]{:S(2)}) %collective-permute-start) | collective-permute-done | bytes 43040 | tf_op jit(solution)/shard_map/ppermute | solution.py:18
  10.8 0.4 collective-permute-done.1
  11.2 1.0 %pad_maximum_fusion = f32[21,104,128]{2,0,1:T(8,128)S(1)} fusion(f32[21,4,128]{2,0,1:T(8,128)} %collective-permute-done.1, f32[1,96,128]{2,0,1:T(1,128)} %bitcast.70, f32[20,96,128]{2,0,1:T(8,128)S(1)} %bitcast.60, f32[21,4,128]{2,0,1:T(8,128)} %collective-permute-done), kind=kLoop, calls=%fused_computation.8 | loop fusion | flops 838656 | bytes 2236416 | tf_op jit(solution)/shard_map/concatenate | solution.py:16
  12.2 0.4 fusion.25
  12.6 0.0 copy-start.3
  12.6 0.4 fusion.26
  13.0 0.4 copy-done.3
  13.4 0.8 %pad_maximum_fusion.1 = f32[1,102,128]{2,0,1:T(1,128)S(1)} fusion(f32[21,4,128]{2,0,1:T(8,128)} %collective-permute-done.1, f32[21,4,128]{2,0,1:T(8,128)} %collective-permute-done, f32[1,96,128]{2,0,1:T(1,128)S(1)} %bitcast.72, f32[20,96,128]{2,0,1:T(8,128)S(1)} %bitcast.61), kind=kLoop, calls=%fused_computation.38 | loop fusion | flops 39168 | bytes 1170432 | tf_op jit(solution)/shard_map/slice | solution.py:59
  14.2 1.2 %add_select_fusion = f32[20,102,128]{2,0,1:T(8,128)S(1)} fusion(f32[21,104,128]{2,0,1:T(8,128)S(1)} %pad_maximum_fusion, f32[20,102,127]{2,0,1:T(8,128)S(1)} %get-tuple-element.3, f32[20,102,1]{2,0,1:T(8,128)S(1)} %get-tuple-element.5, f32[20,102,1]{2,0,1:T(8,128)S(1)} %get-tuple-element.4, f32[20,102,127]{2,0,1:T(8,128)S(1)} %get-tuple-element.2, ...), kind=kLoop, calls=%fused_computation.3 | loop fusion | flops 2611200 | bytes 6319105 | tf_op jit(solution)/shard_map/jit(_where)/select_n | solution.py:67
  15.4 0.4 fusion.28
  15.8 0.4 fusion.27
  16.2 0.8 %pad_maximum_fusion.2 = f32[1,100,128]{2,0,1:T(1,128)S(1)} fusion(f32[21,4,128]{2,0,1:T(8,128)} %collective-permute-done.1, f32[21,4,128]{2,0,1:T(8,128)} %collective-permute-done, f32[1,96,128]{2,0,1:T(1,128)S(1)} %bitcast.73, f32[20,96,128]{2,0,1:T(8,128)S(1)} %bitcast.62), kind=kLoop, calls=%fused_computation.39 | loop fusion | flops 38400 | bytes 1169408 | tf_op jit(solution)/shard_map/slice | solution.py:59
  17.1 1.2 %add_select_fusion.1 = f32[20,100,128]{2,0,1:T(8,128)S(1)} fusion(f32[20,102,128]{2,0,1:T(8,128)S(1)} %add_select_fusion, f32[20,100,127]{2,0,1:T(8,128)S(1)} %get-tuple-element.7, f32[20,100,1]{2,0,1:T(8,128)S(1)} %get-tuple-element.9, f32[20,100,1]{2,0,1:T(8,128)S(1)} %get-tuple-element.8, f32[20,100,127]{2,0,1:T(8,128)S(1)} %get-tuple-element.6, ...), kind=kLoop, calls=%fused_computation.4 | loop fusion | flops 2560000 | bytes 6195201 | tf_op jit(solution)/shard_map/jit(_where)/select_n | solution.py:67
  18.3 0.4 fusion.30
  18.6 0.4 fusion.29
  19.0 0.8 pad_maximum_fusion.3
  19.8 1.2 %add_select_fusion.2 = f32[20,98,128]{2,0,1:T(8,128)S(1)} fusion(f32[20,100,128]{2,0,1:T(8,128)S(1)} %add_select_fusion.1, f32[20,98,127]{2,0,1:T(8,128)S(1)} %get-tuple-element.11, f32[20,98,1]{2,0,1:T(8,128)S(1)} %get-tuple-element.13, f32[20,98,1]{2,0,1:T(8,128)S(1)} %get-tuple-element.12, f32[20,98,127]{2,0,1:T(8,128)S(1)} %get-tuple-element.10, ...), kind=kLoop, calls=%fused_computation.5 | loop fusion | flops 2508800 | bytes 6071297 | tf_op jit(solution)/shard_map/jit(_where)/select_n | solution.py:67
  21.0 0.4 fusion.32
  21.4 0.4 fusion.31
  21.8 2.2 %add_select_fusion.3 = f32[20,96,128]{2,0,1:T(8,128)} fusion(f32[20,98,128]{2,0,1:T(8,128)S(1)} %add_select_fusion.2, f32[20,96,127]{2,0,1:T(8,128)S(1)} %get-tuple-element.17, f32[20,96,1]{2,0,1:T(8,128)S(1)} %get-tuple-element.19, f32[20,96,1]{2,0,1:T(8,128)S(1)} %get-tuple-element.18, f32[20,96,127]{2,0,1:T(8,128)S(1)} %get-tuple-element.16, ...), kind=kLoop, calls=%fused_computation.6 | loop fusion | flops 2457600 | bytes 5947393 | tf_op jit(solution)/shard_map/jit(_where)/select_n | solution.py:67
  23.9 3.8 %all-to-all-start = ((f32[20,96,128]{2,0,1:T(8,128)}), f32[20,96,128]{2,0,1:T(8,128)S(1)}, u32[]{:S(2)}, u32[]{:S(2)}) async-start(f32[20,96,128]{2,0,1:T(8,128)} %add_select_fusion.3), calls=%async_computation | async-start | bytes 2359296 | tf_op jit(solution)/shard_map/all_to_all | solution.py:69
  27.8 0.0 copy-done.9
  27.8 0.7 iota_compare_fusion
  28.5 13.1 %all-to-all-done = f32[20,96,128]{2,0,1:T(8,128)S(1)} async-done(((f32[20,96,128]{2,0,1:T(8,128)}), f32[20,96,128]{2,0,1:T(8,128)S(1)}, u32[]{:S(2)}, u32[]{:S(2)}) %all-to-all-start) | async-done | bytes 983072 | tf_op jit(solution)/shard_map/all_to_all | solution.py:69
  41.5 0.2 copy.25
  41.7 0.7 fusion.20
  42.4 0.6 convert_element_type.9
  43.0 0.0 collective-permute-start.2
  43.0 0.1 copy.26
  43.1 0.6 reshape.105
  43.7 0.8 collective-permute-done.2
  44.5 1.2 %fusion.33 = (bf16[8,128]{1,0:T(8,128)(2,1)}, bf16[8,128]{1,0:T(8,128)(2,1)}) fusion(bf16[24,128]{1,0:T(8,128)(2,1)} %collective-permute-done.2), kind=kLoop, calls=%fused_computation.61 | loop fusion | bytes 8192 | tf_op jit(solution)/shard_map/slice | solution.py:15
  45.8 1.4 %collective-permute-start.3 = (bf16[8,128]{1,0:T(8,128)(2,1)}, bf16[8,128]{1,0:T(8,128)(2,1)}, u32[]{:S(2)}, u32[]{:S(2)}) collective-permute-start(bf16[8,128]{1,0:T(8,128)(2,1)} %get-tuple-element.20), channel_id=1, source_target_pairs={{0,1},{1,2},{2,3},{3,4},{4,5},{5,6},{6,7},{7,8},{8,9},{9,10},{10,1... | collective-permute-start | bytes 6152 | tf_op jit(solution)/shard_map/ppermute | solution.py:18
  47.2 4.2 %collective-permute-start.4 = (bf16[8,128]{1,0:T(8,128)(2,1)}, bf16[8,128]{1,0:T(8,128)(2,1)}, u32[]{:S(2)}, u32[]{:S(2)}) collective-permute-start(bf16[8,128]{1,0:T(8,128)(2,1)} %get-tuple-element.21), channel_id=1, source_target_pairs={{1,0},{2,1},{3,2},{4,3},{5,4},{6,5},{7,6},{8,7},{9,8},{10,9},{11,1... | collective-permute-start | bytes 6152 | tf_op jit(solution)/shard_map/ppermute | solution.py:20
  51.4 0.7 pad_clamp_fusion
  52.0 0.5 broadcast.93
  52.6 1.3 %reduce.3 = f32[80]{0:T(128)S(1)} reduce(f32[1,80]{1,0:T(1,128)} %param.16, f32[]{:T(128)} %broadcast.93), dimensions={0}, to_apply=%param.16.reduce_sub_computation.3 | reduce | bytes 644 | tf_op args[7]
  53.9 0.7 mul.110
  54.5 0.8 copy.24
  55.3 1.1 %copy.23 = f32[20,96,128]{2,1,0:T(8,128)} copy(f32[20,96,128]{2,0,1:T(8,128)S(1)} %all-to-all-done) | data formatting | bytes 1966080 | tf_op jit(solution)/shard_map/all_to_all | solution.py:69
  56.4 0.0 collective-permute-done.3
  56.4 0.0 collective-permute-done.4
  56.4 0.7 pad_maximum_fusion.6
  57.1 0.6 gather_fusion
  57.8 0.0 copy-start.6
  57.8 0.8 select_bitcast_fusion
  58.6 0.0 copy-start.1
  58.6 0.5 fusion
  59.2 0.6 copy-done.1
  59.8 0.2 multiply_add_fusion
  60.0 0.0 copy-start.5
  60.0 0.1 copy.27
  60.1 0.7 copy-done.5
  60.7 1.1 %convolution_bitcast_fusion = f32[10,8,24,128]{3,1,2,0:T(8,128)S(1)} fusion(f32[10,8,24,128]{3,2,1,0:T(8,128)S(1)} %bitcast.66, f32[1,80,80]{2,1,0:T(8,128)S(1)} %copy-done.5), kind=kOutput, calls=%fused_computation.7 | convolution fusion | flops 235929600 | bytes 1991680 | tf_op jit(solution)/shard_map/dot_general | solution.py:90
  61.8 0.2 copy.38
  62.0 16.1 %all_to_all.33 = f32[80,24,128]{2,1,0:T(8,128)S(1)} all-to-all(f32[80,24,128]{2,1,0:T(8,128)S(1)} %bitcast.67), channel_id=1, replica_groups=mesh['sec'=2,'horiz'=4,'lev'=4] {'lev'}, dimensions={0} | all-to-all | bytes 1966080 | tf_op jit(solution)/shard_map/all_to_all | solution.py:97
  78.1 1.1 %copy.28 = f32[4,20,24,128]{3,2,0,1:T(8,128)} copy(f32[4,20,24,128]{3,2,1,0:T(8,128)S(1)} %bitcast.68) | data formatting | bytes 1966080 | tf_op jit(solution)/shard_map/all_to_all | solution.py:97
  (15 shorter events, 0.1 us)
Async XLA Ops:
  0.6 58.0 %copy-start = (bf16[1,24,3,128,128]{4,3,2,1,0:T(8,128)(2,1)S(1)}, bf16[1,24,3,128,128]{4,3,2,1,0:T(8,128)(2,1)}, u32[]{:S(2)}) copy-start(bf16[1,24,3,128,128]{4,3,2,1,0:T(8,128)(2,1)} %param.14) | copy-start | bytes 7077892
  0.6 2.0 %copy-start.2 = (f32[1,96,128]{2,1,0:T(8,128)S(1)}, f32[1,96,128]{2,1,0:T(8,128)}, u32[]{:S(2)}) copy-start(f32[1,96,128]{2,1,0:T(8,128)} %param.10) | copy-start | bytes 147460
  3.3 7.5 %collective-permute-start = (f32[21,4,128]{2,0,1:T(8,128)}, f32[21,4,128]{2,0,1:T(8,128)}, u32[]{:S(2)}, u32[]{:S(2)}) collective-permute-start(f32[21,4,128]{2,0,1:T(8,128)} %get-tuple-element.14), channel_id=1, source_target_pairs={{0,4},{4,8},{8,12},{12,0},{1,5},{5,9},{9,13},{13,1},{2,6},{6,10},{... | collective-permute-start | bytes 129032 | tf_op jit(solution)/shard_map/ppermute | solution.py:18
  6.3 4.9 %collective-permute-start.1 = (f32[21,4,128]{2,0,1:T(8,128)}, f32[21,4,128]{2,0,1:T(8,128)}, u32[]{:S(2)}, u32[]{:S(2)}) collective-permute-start(f32[21,4,128]{2,0,1:T(8,128)} %get-tuple-element.15), channel_id=1, source_target_pairs={{4,0},{8,4},{12,8},{0,12},{5,1},{9,5},{13,9},{1,13},{6,2},{10,6},{... | collective-permute-start | bytes 129032 | tf_op jit(solution)/shard_map/ppermute | solution.py:20
  12.6 0.8 %copy-start.3 = (f32[1,96,128]{2,1,0:T(8,128)S(1)}, f32[1,96,128]{2,1,0:T(8,128)}, u32[]{:S(2)}) copy-start(f32[1,96,128]{2,1,0:T(8,128)} %param.10) | copy-start | bytes 147460
  23.9 3.9 %copy-start.9 = (s32[1,24]{1,0:T(1,128)S(1)}, s32[1,24]{1,0:T(1,128)}, u32[]{:S(2)}) copy-start(s32[1,24]{1,0:T(1,128)} %param.13) | copy-start | bytes 292
  23.9 17.6 %all-to-all-start = ((f32[20,96,128]{2,0,1:T(8,128)}), f32[20,96,128]{2,0,1:T(8,128)S(1)}, u32[]{:S(2)}, u32[]{:S(2)}) async-start(f32[20,96,128]{2,0,1:T(8,128)} %add_select_fusion.3), calls=%async_computation | async-start | bytes 2359296 | tf_op jit(solution)/shard_map/all_to_all | solution.py:69
  27.8 13.9 %copy-start.8 = (f32[1,80]{1,0:T(1,128)S(1)}, f32[1,80]{1,0:T(1,128)}, u32[]{:S(2)}) copy-start(f32[1,80]{1,0:T(1,128)} %param.15) | copy-start | bytes 964
  41.5 1.5 %copy-start.7 = (s32[1,24,3]{1,0,2:T(1,128)S(1)}, s32[1,24,3]{1,0,2:T(1,128)}, u32[]{:S(2)}) copy-start(s32[1,24,3]{1,0,2:T(1,128)} %param.12) | copy-start | bytes 868
  43.0 1.5 %collective-permute-start.2 = (bf16[24,128]{1,0:T(8,128)(2,1)}, bf16[24,128]{1,0:T(8,128)(2,1)}, u32[]{:S(2)}, u32[]{:S(2)}) collective-permute-start(bf16[24,128]{1,0:T(8,128)(2,1)} %convert_element_type.9), channel_id=1, source_target_pairs={{0,16},{16,0},{1,17},{17,1},{2,18},{18,2},{3,19},{19,3},{4,20},{20... | collective-permute-start | bytes 18440 | tf_op jit(solution)/shard_map/ppermute | solution.py:34
  45.8 10.7 %collective-permute-start.3 = (bf16[8,128]{1,0:T(8,128)(2,1)}, bf16[8,128]{1,0:T(8,128)(2,1)}, u32[]{:S(2)}, u32[]{:S(2)}) collective-permute-start(bf16[8,128]{1,0:T(8,128)(2,1)} %get-tuple-element.20), channel_id=1, source_target_pairs={{0,1},{1,2},{2,3},{3,4},{4,5},{5,6},{6,7},{7,8},{8,9},{9,10},{10,1... | collective-permute-start | bytes 6152 | tf_op jit(solution)/shard_map/ppermute | solution.py:18
  47.2 9.3 %collective-permute-start.4 = (bf16[8,128]{1,0:T(8,128)(2,1)}, bf16[8,128]{1,0:T(8,128)(2,1)}, u32[]{:S(2)}, u32[]{:S(2)}) collective-permute-start(bf16[8,128]{1,0:T(8,128)(2,1)} %get-tuple-element.21), channel_id=1, source_target_pairs={{1,0},{2,1},{3,2},{4,3},{5,4},{6,5},{7,6},{8,7},{9,8},{10,9},{11,1... | collective-permute-start | bytes 6152 | tf_op jit(solution)/shard_map/ppermute | solution.py:20
  57.8 1.3 %copy-start.6 = (s32[1,24,128]{2,1,0:T(8,128)S(1)}, s32[1,24,128]{2,1,0:T(8,128)}, u32[]{:S(2)}) copy-start(s32[1,24,128]{2,1,0:T(8,128)} %param.11) | copy-start | bytes 36868
  58.6 1.2 %copy-start.1 = (f32[20,96,128]{2,1,0:T(8,128)S(1)}, f32[20,96,128]{2,1,0:T(8,128)}, u32[]{:S(2)}) copy-start(f32[20,96,128]{2,1,0:T(8,128)} %copy.23) | copy-start | bytes 2949124
  59.1 0.9 %copy-start.4 = (f32[24,1,128,1]{2,1,3,0:T(1,128)}, f32[24,1,128,1]{2,1,3,0:T(1,128)S(1)}, u32[]{:S(2)}) copy-start(f32[24,1,128,1]{2,1,3,0:T(1,128)S(1)} %fusion) | copy-start | bytes 36868
  60.0 0.8 copy-start.5
where the time goes:
time: 79.9 us; the launch traced here: 79.2 us
  waiting for transfers between devices  16.8 us (21%)
  blocking collectives  16.1 us (20%)
  other arithmetic  14.7 us (18%)
  starting transfers between devices  14.5 us (18%)
  local copies, waits for them, and re-layouts  13.9 us (17%)
  matrix products  2.31 us (3%)
  between operations  0.91 us (1%)
    all_to_all x1, blocking collectives, per_device(): lax.all_to_all(mixed_columns, 'lev', split_axis=0, concat_axis=1, tiled=T...  16.1 us
    all_to_all x1, waiting for transfers between devices, per_device(): lax.all_to_all(current, 'lev', split_axis=1, concat_axis=0, tiled=True)  13.1 us
    ppermute x2, starting transfers between devices, padded(): lax.ppermute(head, axis, [((i + 1) % count, i) for i in range(count)])  6.23 us
    select_n x4, other arithmetic, per_device(): jnp.where(step_index < steps_here, middle + kappa_mid[None] * stencil, mi...  5.78 us
    ppermute x2, starting transfers between devices, padded(): lax.ppermute(tail, axis, [(i, (i + 1) % count) for i in range(count)])  4.45 us
    unnamed x26, local copies, waits for them, and re-layouts  4.42 us
    all_to_all x1, starting transfers between devices, per_device(): lax.all_to_all(current, 'lev', split_axis=1, concat_axis=0, tiled=True)  3.85 us
    slice x8, local copies, waits for them, and re-layouts, per_device(): jnp.roll(middle, -1, 2)  3.04 us
  transfers between devices with their start and end apart: 6, of which 4 were waited for; matrix products, arithmetic and copies ran while one was open for 8% of the time, Pallas kernels for 0%

commit v1 on v0

v1 whole, which is shorter than its diff:
```python
import functools

import jax
import jax.numpy as jnp
from jax import lax
from jax.experimental import pallas as pl
from jax.experimental.pallas import tpu as pltpu
from jax.sharding import PartitionSpec as P

REACH = 8
ATM_STEPS = 4
OCN_STEPS = 2
HALO = 8
MARGIN = REACH + HALO
F32 = jnp.float32
BF16 = jnp.bfloat16


def diffuse(v, kappas):
    rows = v.shape[0]
    for k in kappas:
        around = (
            pltpu.roll(v, 1, 0)
            + pltpu.roll(v, rows - 1, 0)
            + pltpu.roll(v, 1, 1)
            + pltpu.roll(v, v.shape[1] - 1, 1)
        )
        v = v + k * (around - 4.0 * v)
    return v


def kernel(
    sizes,
    x_ref,
    kap_ref,
    mask_ref,
    rows_ref,
    counts_ref,
    w_hbm,
    exp_ref,
    imp_ref,
    inv_ref,
    out_ref,
    f_ref,
    w_buf,
    p_buf,
    part,
    kapw,
    halo_x,
    halo_k,
    dyn16,
    col16,
    c_buf,
    z_buf,
    y16,
    yr,
    fm,
    cs,
    w_sem,
    halo_s,
    halo_r,
    halok_s,
    halok_r,
    part_s,
    part_r,
    pedge_s,
    pedge_r,
    kapw_s,
    kapw_r,
    kedge_s,
    kedge_r,
    bulk_s,
    bulk_r,
    fm_s,
    fm_r,
    ret_s,
    ret_r,
):
    H, L, K, R, W = sizes
    B = R // L
    T = B // 8
    G = K // 2
    WIN = B + 2 * MARGIN
    LEV = K * L
    s = lax.axis_index("sec")
    h = lax.axis_index("horiz")
    l = lax.axis_index("lev")
    other = 1 - s
    nxt = lax.rem(h + 1, H)
    prv = lax.rem(h + H - 1, H)

    def remote(src, dst, ssem, rsem, dev):
        return pltpu.make_async_remote_copy(
            src_ref=src,
            dst_ref=dst,
            send_sem=ssem,
            recv_sem=rsem,
            device_id=dev,
            device_id_type=pl.DeviceIdType.MESH,
        )

    w_copy = pltpu.make_async_copy(w_hbm, w_buf, w_sem)
    w_copy.start()

    barrier = pltpu.get_barrier_semaphore()

    def greet(dev):
        pl.semaphore_signal(barrier, inc=1, device_id=dev, device_id_type=pl.DeviceIdType.MESH)

    for d in range(1, L):
        greet((s, h, lax.rem(l + d, L)))
    greet((s, nxt, l))
    greet((s, prv, l))
    for q in range(L):
        greet((other, h, q))

    @pl.when(l == 0)
    def _():
        for q in range(L):
            greet((other, prv, q))

    @pl.when(l == L - 1)
    def _():
        for q in range(L):
            greet((other, nxt, q))

    def add_level(k, acc):
        return acc + exp_ref[0, l * K + k] * x_ref[k]

    p_buf[...] = lax.fori_loop(0, K, add_level, jnp.zeros((R, W), F32), unroll=4)

    pl.semaphore_wait(barrier, (L - 1) + 2 + L + 2)

    halos = [
        remote(x_ref.at[:, pl.ds(R - HALO, HALO)], halo_x.at[0], halo_s.at[0], halo_r.at[0], (s, nxt, l)),
        remote(x_ref.at[:, pl.ds(0, HALO)], halo_x.at[1], halo_s.at[1], halo_r.at[1], (s, prv, l)),
        remote(kap_ref.at[pl.ds(R - HALO, HALO)], halo_k.at[0], halok_s.at[0], halok_r.at[0], (s, nxt, l)),
        remote(kap_ref.at[pl.ds(0, HALO)], halo_k.at[1], halok_s.at[1], halok_r.at[1], (s, prv, l)),
    ]
    for c in halos:
        c.start()

    def window(q):
        lo = max(q * B - MARGIN, 0)
        hi = min(q * B + B + MARGIN, R)
        return lo, lo - (q * B - MARGIN), hi - lo

    def part_copy(q):
        lo, at, n = window(q)
        return remote(
            p_buf.at[pl.ds(lo, n)], part.at[l, pl.ds(at, n)], part_s.at[q], part_r.at[l], (other, h, q)
        )

    def kap_copy(q):
        lo, at, n = window(q)
        return remote(kap_ref.at[pl.ds(lo, n)], kapw.at[pl.ds(at, n)], kapw_s, kapw_r, (other, h, q))

    edge_low = remote(
        p_buf.at[pl.ds(R - MARGIN, MARGIN)],
        part.at[l, pl.ds(0, MARGIN)],
        pedge_s.at[0],
        pedge_r.at[l],
        (other, nxt, 0),
    )
    edge_high = remote(
        p_buf.at[pl.ds(0, MARGIN)],
        part.at[l, pl.ds(WIN - MARGIN, MARGIN)],
        pedge_s.at[1],
        pedge_r.at[l],
        (other, prv, L - 1),
    )
    kedge_low = remote(
        kap_ref.at[pl.ds(R - MARGIN, MARGIN)], kapw.at[pl.ds(0, MARGIN)], kedge_s, kedge_r, (other, nxt, 0)
    )
    kedge_high = remote(
        kap_ref.at[pl.ds(0, MARGIN)],
        kapw.at[pl.ds(WIN - MARGIN, MARGIN)],
        kedge_s,
        kedge_r,
        (other, prv, L - 1),
    )
    for q in range(L):
        part_copy(q).start()
    edge_low.start()
    edge_high.start()
    for q in range(L):

        @pl.when(l == q)
        def _(q=q):
            kap_copy(q).start()

    @pl.when(l == 0)
    def _():
        kedge_low.start()

    @pl.when(l == L - 1)
    def _():
        kedge_high.start()

    steps = jnp.where(s == 0, ATM_STEPS, OCN_STEPS)
    steps_other = jnp.where(s == 0, OCN_STEPS, ATM_STEPS)

    def staged(k, count):
        return [k if i < OCN_STEPS else jnp.where(i < count, k, 0.0) for i in range(ATM_STEPS)]

    def keep(v, at, first, g, levels):
        for q, row in levels:
            for t in range(T):
                lo = row + 8 * t - first + at
                dyn16[q, t, g] = jnp.concatenate([v[0][lo : lo + 8], v[1][lo : lo + 8]], axis=0).astype(BF16)

    def bulk_copy(q, dst_slot):
        return remote(dyn16.at[q], col16.at[dst_slot], bulk_s.at[q], bulk_r.at[dst_slot], (s, h, q))

    def send_bulk(q):
        @pl.when(l != q)
        def _():
            bulk_copy(q, l).start()

        @pl.when(l == q)
        def _():
            col16[q] = dyn16[q]

    lo_c, hi_c = B - HALO, R - B + HALO
    k_mid = staged(kap_ref[lo_c:hi_c], steps)

    def middle(g, _):
        v = [diffuse(x_ref[2 * g + e, lo_c:hi_c, :], k_mid) for e in range(2)]
        for e in range(2):
            out_ref[2 * g + e, B : R - B, :] = v[e][HALO : HALO + R - 2 * B]
        keep(v, 0, lo_c, g, [(q, q * B) for q in range(1, L - 1)])
        return 0

    lax.fori_loop(0, G, middle, 0)
    for q in range(1, L - 1):
        send_bulk(q)

    for c in halos:
        c.wait_recv()

    k_top = staged(jnp.concatenate([halo_k[0], kap_ref[0 : B + HALO]], axis=0), steps)

    def top(g, _):
        v = [
            diffuse(jnp.concatenate([halo_x[0, 2 * g + e], x_ref[2 * g + e, 0 : B + HALO, :]], axis=0), k_top)
            for e in range(2)
        ]
        for e in range(2):
            out_ref[2 * g + e, 0:B, :] = v[e][HALO : HALO + B]
        keep(v, HALO, 0, g, [(0, 0)])
        return 0

    lax.fori_loop(0, G, top, 0)
    send_bulk(0)

    k_bot = staged(jnp.concatenate([kap_ref[R - B - HALO : R], halo_k[1]], axis=0), steps)

    def bottom(g, _):
        v = [
            diffuse(
                jnp.concatenate([x_ref[2 * g + e, R - B - HALO : R, :], halo_x[1, 2 * g + e]], axis=0), k_bot
            )
            for e in range(2)
        ]
        for e in range(2):
            out_ref[2 * g + e, R - B : R, :] = v[e][HALO : HALO + B]
        keep(v, HALO, R - B, g, [(L - 1, R - B)])
        return 0

    lax.fori_loop(0, G, bottom, 0)
    send_bulk(L - 1)

    inv = inv_ref[...]
    first = lax.broadcasted_iota(jnp.int32, (LEV, LEV), 0)
    second = lax.broadcasted_iota(jnp.int32, (LEV, LEV), 1)
    mix = inv - jnp.where(first == second, 1.0, 0.0)
    mix_hi = mix.astype(BF16)
    mix_lo = (mix - mix_hi.astype(F32)).astype(BF16)
    cs[...] = jnp.broadcast_to(jnp.sum(inv * imp_ref[...], axis=1, keepdims=True), (LEV, W))

    for q in range(L):
        lo, at, n = window(q)

        @pl.when(l == q)
        def _(q=q, at=at, n=n):
            for p in range(L):
                remote(
                    p_buf.at[pl.ds(0, n)], part.at[p, pl.ds(at, n)], part_s.at[q], part_r.at[p], (other, h, p)
                ).wait_recv()
            remote(kap_ref.at[pl.ds(0, n)], kapw.at[pl.ds(at, n)], kapw_s, kapw_r, (other, h, q)).wait_recv()
            if q == 0 or q == L - 1:
                at_e = 0 if q == 0 else WIN - MARGIN
                for p in range(L):
                    remote(
                        p_buf.at[pl.ds(0, MARGIN)],
                        part.at[p, pl.ds(at_e, MARGIN)],
                        pedge_s.at[0],
                        pedge_r.at[p],
                        (other, h, p),
                    ).wait_recv()
                remote(
                    kap_ref.at[pl.ds(0, MARGIN)], kapw.at[pl.ds(at_e, MARGIN)], kedge_s, kedge_r, (other, h, q)
                ).wait_recv()

    total = part[0]
    for p in range(1, L):
        total = total + part[p]
    surface = diffuse(total, staged(kapw[...], steps_other)).astype(BF16)

    first_row = (h * L + l) * B
    rows_total = H * L * B
    place = rows_ref[...] - first_row + REACH
    place = jnp.where(place < 0, place + rows_total, place)
    place = jnp.where(place >= rows_total, place - rows_total, place) + HALO
    usable = lax.broadcasted_iota(jnp.int32, place.shape, 1) < counts_ref[...]
    place = jnp.where(usable, place, -1)
    cells = lax.broadcasted_iota(jnp.int32, (B, WIN), 1)
    pairs = place.shape[1]
    sources = jnp.concatenate(
        [
            jnp.dot(
                jnp.where(cells == place[:, j : j + 1], 1.0, 0.0).astype(BF16),
                surface,
                preferred_element_type=F32,
            ).astype(BF16)
            for j in range(pairs)
        ],
        axis=1,
    )
    w_copy.wait()
    row_of = lax.broadcasted_iota(jnp.int32, (B, W), 0)
    forcing = jnp.zeros((B, W), F32)
    for r in range(B):
        product = jnp.dot(sources, w_buf[r * pairs * W : (r + 1) * pairs * W, :], preferred_element_type=F32)
        forcing = jnp.where(row_of == r, product, forcing)
    f_ref[...] = forcing
    fm[l] = forcing * mask_ref[...].astype(F32)

    def fm_copy(d, slot):
        peer = lax.rem(l + d, L)
        return remote(fm.at[slot], fm.at[slot], fm_s.at[d - 1], fm_r.at[slot], (s, h, peer))

    for d in range(1, L):
        fm_copy(d, l).start()

    for q in range(L):

        @pl.when(l != q)
        def _(q=q):
            bulk_copy(q, q).wait_recv()

    def ret_copy(q, t, slot):
        return remote(y16.at[q, t], yr.at[slot, t], ret_s.at[q, t], ret_r.at[slot, t], (s, h, q))

    for t in range(T):
        for q in range(L):
            c_buf[t, q * K * 8 : (q + 1) * K * 8, :] = col16[q, t].astype(F32).reshape(K * 8, W)
        for r in range(0, 8, 2):
            x = jnp.concatenate(
                [c_buf[t, pl.ds(r + e, LEV, stride=8), :] for e in range(2)], axis=1
            ).astype(BF16)
            y = jnp.dot(mix_hi, x, preferred_element_type=F32) + jnp.dot(
                mix_lo, x, preferred_element_type=F32
            )
            for e in range(2):
                z_buf[t, pl.ds(r + e, LEV, stride=8), :] = y[:, e * W : (e + 1) * W]
        for q in range(L):
            y16[q, t] = z_buf[t, q * K * 8 : (q + 1) * K * 8, :].reshape(G, 16, W).astype(BF16)
        for q in range(L):

            @pl.when(l != q)
            def _(q=q, t=t):
                ret_copy(q, t, l).start()

            @pl.when(l == q)
            def _(q=q, t=t):
                yr[q, t] = y16[q, t]

    for d in range(1, L):
        fm_copy(d, lax.rem(l + d, L)).wait_recv()

    for t in range(T):
        for q in range(L):

            @pl.when(l != q)
            def _(q=q, t=t):
                ret_copy(q, t, q).wait_recv()

        def finish(g, _, t=t):
            for e in range(2):
                k = 2 * g + e
                c = cs[pl.ds(l * K + k, 1), :]
                for q in range(L):
                    at = q * B + 8 * t
                    y = yr[q, t, g].astype(F32)[8 * e : 8 * e + 8]
                    out_ref[k, at : at + 8, :] = out_ref[k, at : at + 8, :] + (
                        y + c * fm[q, 8 * t : 8 * t + 8, :]
                    )
            return 0

        lax.fori_loop(0, G, finish, 0)

    for c in halos:
        c.wait_send()
    for q in range(L):
        part_copy(q).wait_send()

        @pl.when(l == q)
        def _(q=q):
            kap_copy(q).wait_send()

        @pl.when(l != q)
        def _(q=q):
            bulk_copy(q, l).wait_send()
            for t in range(T):
                ret_copy(q, t, l).wait_send()

    edge_low.wait_send()
    edge_high.wait_send()

    @pl.when(l == 0)
    def _():
        kedge_low.wait_send()

    @pl.when(l == L - 1)
    def _():
        kedge_high.wait_send()

    for d in range(1, L):
        fm_copy(d, l).wait_send()


def per_device(
    state,
    diffusivity,
    coupling_mask,
    pair_rows,
    pair_counts,
    remap_weights,
    export_profile,
    import_profile,
    column_inverse,
):
    _, K, R, W = state.shape
    H = lax.axis_size("horiz")
    L = lax.axis_size("lev")
    B = R // L
    T = B // 8
    G = K // 2
    WIN = B + 2 * MARGIN
    LEV = K * L
    pairs = pair_rows.shape[2]
    weights = remap_weights.reshape(B * pairs * W, W)
    vmem = pl.BlockSpec(memory_space=pltpu.VMEM)
    smem = pl.BlockSpec(memory_space=pltpu.SMEM)
    hbm = pl.BlockSpec(memory_space=pl.ANY)
    dma = pltpu.SemaphoreType.DMA
    new_state, forcing = pl.pallas_call(
        functools.partial(kernel, (H, L, K, R, W)),
        out_shape=(jax.ShapeDtypeStruct((K, R, W), F32), jax.ShapeDtypeStruct((B, W), F32)),
        in_specs=[vmem, vmem, vmem, vmem, vmem, hbm, smem, vmem, vmem],
        out_specs=(vmem, vmem),
        scratch_shapes=[
            pltpu.VMEM(weights.shape, BF16),
            pltpu.VMEM((R, W), F32),
            pltpu.VMEM((L, WIN, W), F32),
            pltpu.VMEM((WIN, W), F32),
            pltpu.VMEM((2, K, HALO, W), F32),
            pltpu.VMEM((2, HALO, W), F32),
            pltpu.VMEM((L, T, G, 16, W), BF16),
            pltpu.VMEM((L, T, G, 16, W), BF16),
            pltpu.VMEM((T, LEV * 8, W), F32),
            pltpu.VMEM((T, LEV * 8, W), F32),
            pltpu.VMEM((L, T, G, 16, W), BF16),
            pltpu.VMEM((L, T, G, 16, W), BF16),
            pltpu.VMEM((L, B, W), F32),
            pltpu.VMEM((LEV, W), F32),
            dma,
            dma((2,)),
            dma((2,)),
            dma((2,)),
            dma((2,)),
            dma((L,)),
            dma((L,)),
            dma((2,)),
            dma((L,)),
            dma,
            dma,
            dma,
            dma,
            dma((L,)),
            dma((L,)),
            dma((L - 1,)),
            dma((L,)),
            dma((L, T)),
            dma((L, T)),
        ],
        compiler_params=pltpu.CompilerParams(
            collective_id=0, has_side_effects=True, vmem_limit_bytes=40 * 1024 * 1024
        ),
    )(
        state[0],
        diffusivity[0],
        coupling_mask[0],
        pair_rows[0],
        pair_counts.reshape(B, 1),
        weights,
        export_profile,
        import_profile,
        column_inverse[0],
    )
    return (new_state[None], forcing[None])


def solution(mesh):
    placed = (
        P("sec", "lev", "horiz", None),
        P("sec", "horiz", None),
        P("sec", ("horiz", "lev"), None),
        P("sec", ("horiz", "lev"), None),
        P("sec", ("horiz", "lev")),
        P("sec", ("horiz", "lev"), None, None, None),
        P("sec", None),
        P("sec", None),
        P("sec", None, None),
    )
    return jax.shard_map(
        per_device,
        mesh=mesh,
        in_specs=placed,
        out_specs=(P("sec", "lev", "horiz", None), P("sec", ("horiz", "lev"), None)),
        check_vma=False,
    )
```

time: 79.9 us -> 45.2 us (0.57)
  Pallas kernels: 0 us -> 34.7 us
  waiting for transfers between devices: 16.8 us -> 0 us
  blocking collectives: 16.1 us -> 0 us
  other arithmetic: 14.7 us -> 0 us
  starting transfers between devices: 14.5 us -> 0 us
  local copies, waits for them, and re-layouts: 13.9 us -> 9.5 us
  matrix products: 2.31 us -> 0 us
    pallas_call x0 -> x1, Pallas kernels: none -> 34.7 us  [per_device(): pl.pallas_call(functools.partial(kernel, (H, L, K, R, W)), out_shape=(jax...]
    all_to_all x1 -> x0, blocking collectives: 16.1 us -> none  [per_device(): lax.all_to_all(mixed_columns, 'lev', split_axis=0, concat_axis=1, tiled=T...]
    all_to_all x1 -> x0, waiting for transfers between devices: 13.1 us -> none  [per_device(): lax.all_to_all(current, 'lev', split_axis=1, concat_axis=0, tiled=True)]
    ppermute x5 -> x0, starting transfers between devices: 10.7 us -> none  [the longest x2 6.23 us: padded(): lax.ppermute(head, axis, [((i + 1) % count, i) for i in range(count)])]
    select_n x6 -> x0, other arithmetic: 6.57 us -> none  [the longest x4 5.78 us: per_device(): jnp.where(step_index < steps_here, middle + kappa_mid[None] * stencil, mi...]
    slice x9 -> x0, local copies, waits for them, and re-layouts: 4.29 us -> none  [the longest x8 3.04 us: per_device(): jnp.roll(middle, -1, 2)]
    all_to_all x1 -> x0, starting transfers between devices: 3.85 us -> none  [per_device(): lax.all_to_all(current, 'lev', split_axis=1, concat_axis=0, tiled=True)]
    ppermute x5 -> x0, waiting for transfers between devices: 3.7 us -> none  [the longest x2 2.49 us: padded(): lax.ppermute(tail, axis, [(i, (i + 1) % count) for i in range(count)])]
  transfers between devices with their start and end apart: 6 -> 0, of which waited for: 4 -> 0; matrix products, arithmetic and copies ran while one was open for 8% -> 0% of each run, Pallas kernels for 0% -> 0%
where the time goes in v1:
time: 45.2 us; the launch traced here: 44.8 us
  Pallas kernels  34.7 us (77%)
  local copies, waits for them, and re-layouts  9.5 us (21%)
  between operations  0.65 us (1%)
    pallas_call x1, Pallas kernels, per_device(): pl.pallas_call(functools.partial(kernel, (H, L, K, R, W)), out_shape=(jax...  34.7 us
    unnamed x16, local copies, waits for them, and re-layouts  8 us

profile of v1, /device:TPU:0, one launch (start us, length us, event | category | flops | bytes accessed | tf_op | source)
XLA Modules:
  0.0 44.8 jit_solution(14197454846395922145)
XLA Ops:
  0.6 0.8 %copy.13 = s32[1,24,3]{2,1,0:T(8,128)S(1)} copy(s32[1,24,3]{1,0,2:T(1,128)} %param.12) | data formatting | bytes 576 | tf_op jit(solution)/shard_map/squeeze | solution.py:505
  1.4 0.7 %copy.12.counts_ref = s32[24,1]{1,0:T(8,128)S(1)} copy(s32[24,1]{0,1:T(1,128)} %bitcast.17) | data formatting | bytes 192 | tf_op jit(solution)/shard_map/reshape | solution.py:506
  2.1 0.0 copy-start
  2.1 1.7 %copy-done = bf16[1,24,3,128,128]{4,3,2,1,0:T(8,128)(2,1)S(1)} copy-done((bf16[1,24,3,128,128]{4,3,2,1,0:T(8,128)(2,1)S(1)}, bf16[1,24,3,128,128]{4,3,2,1,0:T(8,128)(2,1)}, u32[]{:S(2)}) %copy-start) | copy-done | bytes 2359320
  3.8 0.0 copy-start.1
  3.8 1.2 %copy-done.1 = f32[1,20,96,128]{3,2,1,0:T(8,128)S(1)} copy-done((f32[1,20,96,128]{3,2,1,0:T(8,128)S(1)}, f32[1,20,96,128]{3,2,1,0:T(8,128)}, u32[]{:S(2)}) %copy-start.1) | copy-done | bytes 983064
  5.0 0.0 copy-start.2
  5.0 0.8 %copy-done.2 = f32[1,96,128]{2,1,0:T(8,128)S(1)} copy-done((f32[1,96,128]{2,1,0:T(8,128)S(1)}, f32[1,96,128]{2,1,0:T(8,128)}, u32[]{:S(2)}) %copy-start.2) | copy-done | bytes 49176
  5.8 0.0 copy-start.3
  5.8 0.8 %copy-done.3 = f32[1,80,80]{2,1,0:T(8,128)S(1)} copy-done((f32[1,80,80]{2,1,0:T(8,128)S(1)}, f32[1,80,80]{2,1,0:T(8,128)}, u32[]{:S(2)}) %copy-start.3) | copy-done | bytes 25624
  6.6 0.0 copy-start.4
  6.6 0.7 %copy-done.4 = s32[1,24,128]{2,1,0:T(8,128)S(1)} copy-done((s32[1,24,128]{2,1,0:T(8,128)S(1)}, s32[1,24,128]{2,1,0:T(8,128)}, u32[]{:S(2)}) %copy-start.4) | copy-done | bytes 12312
  7.3 0.0 copy-start.5
  7.3 0.7 %copy-done.5 = f32[1,80]{1,0:T(1,128)S(1)} copy-done((f32[1,80]{1,0:T(1,128)S(1)}, f32[1,80]{1,0:T(1,128)}, u32[]{:S(2)}) %copy-start.5) | copy-done | bytes 344
  7.9 0.0 copy-start.6
  7.9 0.7 %copy-done.6 = f32[1,80]{1,0:T(1,128)S(1)} copy-done((f32[1,80]{1,0:T(1,128)S(1)}, f32[1,80]{1,0:T(1,128)}, u32[]{:S(2)}) %copy-start.6) | copy-done | bytes 344
  8.6 34.7 %shard_map.104 = (f32[20,96,128]{2,1,0:T(8,128)S(1)}, f32[24,128]{1,0:T(8,128)S(1)}) custom-call(f32[20,96,128]{2,1,0:T(8,128)S(1)} %bitcast.10, f32[96,128]{1,0:T(8,128)S(1)} %bitcast.13, s32[24,128]{1,0:T(8,128)S(1)} %bitcast.15, s32[24,3]{1,0:T(8,128)S(1)} %bitcast.12, s32[24,1]{1,0:T(8,128)S(1)} %copy.12.counts_ref, bf16[9216,128]{1,0:T(8,128)(2,1)S(1)} %bitcast.9, ...), custom_call_target="tpu_custom_call" | custom-call | tf_op jit(solution)/shard_map/pallas_call | solution.py:458
  43.3 0.9 %copy.16 = f32[1,20,96,128]{3,2,1,0:T(8,128)} copy(f32[1,20,96,128]{3,2,1,0:T(8,128)S(1)} %bitcast.11) | data formatting | bytes 1966080
  44.2 0.6 %copy.17 = f32[1,24,128]{2,1,0:T(8,128)} copy(f32[1,24,128]{2,1,0:T(8,128)S(1)} %bitcast.16) | data formatting | bytes 24576
Async XLA Ops:
  2.1 1.7 %copy-start = (bf16[1,24,3,128,128]{4,3,2,1,0:T(8,128)(2,1)S(1)}, bf16[1,24,3,128,128]{4,3,2,1,0:T(8,128)(2,1)}, u32[]{:S(2)}) copy-start(bf16[1,24,3,128,128]{4,3,2,1,0:T(8,128)(2,1)} %param.14) | copy-start | bytes 7077892
  3.8 1.2 %copy-start.1 = (f32[1,20,96,128]{3,2,1,0:T(8,128)S(1)}, f32[1,20,96,128]{3,2,1,0:T(8,128)}, u32[]{:S(2)}) copy-start(f32[1,20,96,128]{3,2,1,0:T(8,128)} %param.9) | copy-start | bytes 2949124
  5.0 0.8 %copy-start.2 = (f32[1,96,128]{2,1,0:T(8,128)S(1)}, f32[1,96,128]{2,1,0:T(8,128)}, u32[]{:S(2)}) copy-start(f32[1,96,128]{2,1,0:T(8,128)} %param.10) | copy-start | bytes 147460
  5.8 0.8 %copy-start.3 = (f32[1,80,80]{2,1,0:T(8,128)S(1)}, f32[1,80,80]{2,1,0:T(8,128)}, u32[]{:S(2)}) copy-start(f32[1,80,80]{2,1,0:T(8,128)} %param.17) | copy-start | bytes 76804
  6.6 0.7 %copy-start.4 = (s32[1,24,128]{2,1,0:T(8,128)S(1)}, s32[1,24,128]{2,1,0:T(8,128)}, u32[]{:S(2)}) copy-start(s32[1,24,128]{2,1,0:T(8,128)} %param.11) | copy-start | bytes 36868
  7.3 0.7 %copy-start.5 = (f32[1,80]{1,0:T(1,128)S(1)}, f32[1,80]{1,0:T(1,128)}, u32[]{:S(2)}) copy-start(f32[1,80]{1,0:T(1,128)} %exp_ref.1) | copy-start | bytes 964
  7.9 0.7 %copy-start.6 = (f32[1,80]{1,0:T(1,128)S(1)}, f32[1,80]{1,0:T(1,128)}, u32[]{:S(2)}) copy-start(f32[1,80]{1,0:T(1,128)} %imp_ref.1) | copy-start | bytes 964

commit v2 on v1

--- a/solution.py
+++ b/solution.py
@@ -31,18 +31,26 @@
 
 def kernel(
     sizes,
+    x_hbm,
+    kap_hbm,
+    mask_hbm,
+    rows_hbm,
+    counts_hbm,
+    w_hbm,
+    exp_hbm,
+    imp_hbm,
+    inv_hbm,
+    out_ref,
+    f_ref,
     x_ref,
     kap_ref,
     mask_ref,
     rows_ref,
     counts_ref,
-    w_hbm,
+    w_buf,
     exp_ref,
     imp_ref,
     inv_ref,
-    out_ref,
-    f_ref,
-    w_buf,
     p_buf,
     part,
     kapw,
@@ -56,7 +64,7 @@
     yr,
     fm,
     cs,
-    w_sem,
+    in_sem,
     halo_s,
     halo_r,
     halok_s,
@@ -99,8 +107,24 @@
             device_id_type=pl.DeviceIdType.MESH,
         )
 
-    w_copy = pltpu.make_async_copy(w_hbm, w_buf, w_sem)
-    w_copy.start()
+    loads = [
+        pltpu.make_async_copy(src, dst, in_sem.at[i])
+        for i, (src, dst) in enumerate(
+            (
+                (x_hbm, x_ref),
+                (exp_hbm, exp_ref),
+                (kap_hbm, kap_ref),
+                (inv_hbm, inv_ref),
+                (imp_hbm, imp_ref),
+                (rows_hbm, rows_ref),
+                (counts_hbm, counts_ref),
+                (mask_hbm, mask_ref),
+                (w_hbm, w_buf),
+            )
+        )
+    ]
+    for c in loads:
+        c.start()
 
     barrier = pltpu.get_barrier_semaphore()
 
@@ -124,11 +148,15 @@
         for q in range(L):
             greet((other, nxt, q))
 
+    loads[0].wait()
+    loads[1].wait()
+
     def add_level(k, acc):
         return acc + exp_ref[0, l * K + k] * x_ref[k]
 
     p_buf[...] = lax.fori_loop(0, K, add_level, jnp.zeros((R, W), F32), unroll=4)
 
+    loads[2].wait()
     pl.semaphore_wait(barrier, (L - 1) + 2 + L + 2)
 
     halos = [
@@ -270,6 +298,8 @@
     lax.fori_loop(0, G, bottom, 0)
     send_bulk(L - 1)
 
+    for c in loads[3:8]:
+        c.wait()
     inv = inv_ref[...]
     first = lax.broadcasted_iota(jnp.int32, (LEV, LEV), 0)
     second = lax.broadcasted_iota(jnp.int32, (LEV, LEV), 1)
@@ -312,22 +342,22 @@
     place = rows_ref[...] - first_row + REACH
     place = jnp.where(place < 0, place + rows_total, place)
     place = jnp.where(place >= rows_total, place - rows_total, place) + HALO
-    usable = lax.broadcasted_iota(jnp.int32, place.shape, 1) < counts_ref[...]
-    place = jnp.where(usable, place, -1)
-    cells = lax.broadcasted_iota(jnp.int32, (B, WIN), 1)
-    pairs = place.shape[1]
+    pairs = place.shape[0]
+    counts = counts_ref[...]
+    cells = lax.broadcasted_iota(jnp.int32, (WIN, B), 0)
     sources = jnp.concatenate(
         [
-            jnp.dot(
-                jnp.where(cells == place[:, j : j + 1], 1.0, 0.0).astype(BF16),
+            lax.dot_general(
+                jnp.where((cells == place[j]) & (counts > j), 1.0, 0.0).astype(BF16),
                 surface,
+                (((0,), (0,)), ((), ())),
                 preferred_element_type=F32,
             ).astype(BF16)
             for j in range(pairs)
         ],
         axis=1,
     )
-    w_copy.wait()
+    loads[8].wait()
     row_of = lax.broadcasted_iota(jnp.int32, (B, W), 0)
     forcing = jnp.zeros((B, W), F32)
     for r in range(B):
@@ -452,16 +482,23 @@
     pairs = pair_rows.shape[2]
     weights = remap_weights.reshape(B * pairs * W, W)
     vmem = pl.BlockSpec(memory_space=pltpu.VMEM)
-    smem = pl.BlockSpec(memory_space=pltpu.SMEM)
-    hbm = pl.BlockSpec(memory_space=pl.ANY)
+    hbm = pl.BlockSpec(memory_space=pltpu.HBM)
     dma = pltpu.SemaphoreType.DMA
     new_state, forcing = pl.pallas_call(
         functools.partial(kernel, (H, L, K, R, W)),
         out_shape=(jax.ShapeDtypeStruct((K, R, W), F32), jax.ShapeDtypeStruct((B, W), F32)),
-        in_specs=[vmem, vmem, vmem, vmem, vmem, hbm, smem, vmem, vmem],
+        in_specs=[hbm] * 9,
         out_specs=(vmem, vmem),
         scratch_shapes=[
+            pltpu.VMEM((K, R, W), F32),
+            pltpu.VMEM((R, W), F32),
+            pltpu.VMEM((B, W), jnp.int32),
+            pltpu.VMEM((pairs, 1, B), jnp.int32),
+            pltpu.VMEM((1, B), jnp.int32),
             pltpu.VMEM(weights.shape, BF16),
+            pltpu.SMEM((1, LEV), F32),
+            pltpu.VMEM((1, LEV), F32),
+            pltpu.VMEM((LEV, LEV), F32),
             pltpu.VMEM((R, W), F32),
             pltpu.VMEM((L, WIN, W), F32),
             pltpu.VMEM((WIN, W), F32),
@@ -475,7 +512,7 @@
             pltpu.VMEM((L, T, G, 16, W), BF16),
             pltpu.VMEM((L, B, W), F32),
             pltpu.VMEM((LEV, W), F32),
-            dma,
+            dma((9,)),
             dma((2,)),
             dma((2,)),
             dma((2,)),
@@ -496,14 +533,14 @@
             dma((L, T)),
         ],
         compiler_params=pltpu.CompilerParams(
-            collective_id=0, has_side_effects=True, vmem_limit_bytes=40 * 1024 * 1024
+            collective_id=0, has_side_effects=True, vmem_limit_bytes=56 * 1024 * 1024
         ),
     )(
         state[0],
         diffusivity[0],
         coupling_mask[0],
-        pair_rows[0],
-        pair_counts.reshape(B, 1),
+        jnp.transpose(pair_rows, (2, 0, 1)),
+        pair_counts,
         weights,
         export_profile,
         import_profile,

time: 45.2 us -> 39.3 us (0.87)
  local copies, waits for them, and re-layouts: 9.5 us -> 3.52 us
    unnamed x16 -> x2, local copies, waits for them, and re-layouts: 8 us -> 3.52 us
    squeeze x1 -> x0, local copies, waits for them, and re-layouts: 0.76 us -> none  [per_device(): pair_rows[0]]
    reshape x1 -> x0, local copies, waits for them, and re-layouts: 0.73 us -> none  [per_device(): pair_counts.reshape(B, 1)]
where the time goes in v2:
time: 39.3 us; the launch traced here: 39.1 us
  Pallas kernels  34.9 us (89%)
  local copies, waits for them, and re-layouts  3.52 us (9%)
  between operations  0.64 us (2%)
    pallas_call x1, Pallas kernels, per_device(): pl.pallas_call(functools.partial(kernel, (H, L, K, R, W)), out_shape=(jax...  34.9 us
    unnamed x2, local copies, waits for them, and re-layouts  3.52 us

profile of v2, /device:TPU:0, one launch (start us, length us, event | category | flops | bytes accessed | tf_op | source)
XLA Modules:
  0.0 39.1 jit_solution(2814392489666614999)
XLA Ops:
  0.6 34.9 %shard_map.104 = (f32[20,96,128]{2,1,0:T(8,128)}, f32[24,128]{1,0:T(8,128)}) custom-call(f32[20,96,128]{2,1,0:T(8,128)} %bitcast.9, f32[96,128]{1,0:T(8,128)} %bitcast.11, s32[24,128]{1,0:T(8,128)} %bitcast.13, s32[3,1,24]{2,1,0:T(1,128)} %bitcast.15, s32[1,24]{1,0:T(1,128)} %counts_hbm.1, bf16[9216,128]{1,0:T(8,128)(2,1)} %bitcast.8, f32[1,80]{1,0:T(1,128)} %exp_hbm.1, ...), custom_call_target="tpu_custom_call" | custom-call | tf_op jit(solution)/shard_map/pallas_call | solution.py:487
  35.6 2.2 %copy.13 = f32[1,20,96,128]{3,2,1,0:T(8,128)} copy(f32[1,20,96,128]{3,2,1,0:T(8,128)} %bitcast.10) | data formatting | bytes 1966080
  37.8 1.3 %copy.14 = f32[1,24,128]{2,1,0:T(8,128)} copy(f32[1,24,128]{2,1,0:T(8,128)} %bitcast.14) | data formatting | bytes 24576

commit v3 on v2

--- a/solution.py
+++ b/solution.py
@@ -259,7 +259,7 @@
         keep(v, 0, lo_c, g, [(q, q * B) for q in range(1, L - 1)])
         return 0
 
-    lax.fori_loop(0, G, middle, 0)
+    lax.fori_loop(0, G, middle, 0, unroll=5 if G % 5 == 0 else 1)
     for q in range(1, L - 1):
         send_bulk(q)
 
@@ -278,7 +278,7 @@
         keep(v, HALO, 0, g, [(0, 0)])
         return 0
 
-    lax.fori_loop(0, G, top, 0)
+    lax.fori_loop(0, G, top, 0, unroll=5 if G % 5 == 0 else 1)
     send_bulk(0)
 
     k_bot = staged(jnp.concatenate([kap_ref[R - B - HALO : R], halo_k[1]], axis=0), steps)
@@ -295,7 +295,7 @@
         keep(v, HALO, R - B, g, [(L - 1, R - B)])
         return 0
 
-    lax.fori_loop(0, G, bottom, 0)
+    lax.fori_loop(0, G, bottom, 0, unroll=5 if G % 5 == 0 else 1)
     send_bulk(L - 1)
 
     for c in loads[3:8]:
@@ -486,7 +486,7 @@
     dma = pltpu.SemaphoreType.DMA
     new_state, forcing = pl.pallas_call(
         functools.partial(kernel, (H, L, K, R, W)),
-        out_shape=(jax.ShapeDtypeStruct((K, R, W), F32), jax.ShapeDtypeStruct((B, W), F32)),
+        out_shape=(pltpu.VMEM((K, R, W), F32), pltpu.VMEM((B, W), F32)),
         in_specs=[hbm] * 9,
         out_specs=(vmem, vmem),
         scratch_shapes=[

time: 39.3 us -> 32.4 us (0.82)
  Pallas kernels: 34.9 us -> 30.1 us
  local copies, waits for them, and re-layouts: 3.52 us -> 1.55 us
    pallas_call x1, Pallas kernels: 34.9 us -> 30.1 us  [per_device(): pl.pallas_call(functools.partial(kernel, (H, L, K, R, W)), out_shape=(plt...]
    unnamed x2, local copies, waits for them, and re-layouts: 3.52 us -> 1.55 us
where the time goes in v3:
time: 32.4 us; the launch traced here: 32.3 us
  Pallas kernels  30.1 us (93%)
  local copies, waits for them, and re-layouts  1.55 us (5%)
  between operations  0.64 us (2%)
    pallas_call x1, Pallas kernels, per_device(): pl.pallas_call(functools.partial(kernel, (H, L, K, R, W)), out_shape=(plt...  30.1 us
    unnamed x2, local copies, waits for them, and re-layouts  1.55 us

profile of v3, /device:TPU:0, one launch (start us, length us, event | category | flops | bytes accessed | tf_op | source)
XLA Modules:
  0.0 32.3 jit_solution(4477860353808699519)
XLA Ops:
  0.6 30.1 %shard_map.104 = (f32[20,96,128]{2,1,0:T(8,128)S(1)}, f32[24,128]{1,0:T(8,128)S(1)}) custom-call(f32[20,96,128]{2,1,0:T(8,128)} %bitcast.11, f32[96,128]{1,0:T(8,128)} %bitcast.12, s32[24,128]{1,0:T(8,128)} %bitcast.14, s32[3,1,24]{2,1,0:T(1,128)} %bitcast.15, s32[1,24]{1,0:T(1,128)} %counts_hbm.1, bf16[9216,128]{1,0:T(8,128)(2,1)} %bitcast.10, ...), custom_call_target="tpu_custom_call" | custom-call | tf_op jit(solution)/shard_map/pallas_call | solution.py:487
  30.7 0.9 %copy.13 = f32[1,20,96,128]{3,2,1,0:T(8,128)} copy(f32[1,20,96,128]{3,2,1,0:T(8,128)S(1)} %bitcast.8) | data formatting | bytes 1966080
  31.7 0.6 %copy.14 = f32[1,24,128]{2,1,0:T(8,128)} copy(f32[1,24,128]{2,1,0:T(8,128)S(1)} %bitcast.9) | data formatting | bytes 24576

commit v4 on v3

--- a/solution.py
+++ b/solution.py
@@ -237,17 +237,28 @@
                 lo = row + 8 * t - first + at
                 dyn16[q, t, g] = jnp.concatenate([v[0][lo : lo + 8], v[1][lo : lo + 8]], axis=0).astype(BF16)
 
-    def bulk_copy(q, dst_slot):
-        return remote(dyn16.at[q], col16.at[dst_slot], bulk_s.at[q], bulk_r.at[dst_slot], (s, h, q))
-
-    def send_bulk(q):
+    half = G // 2 if G % 2 == 0 else G
+    parts = G // half
+
+    def bulk_copy(q, dst_slot, i):
+        piece = pl.ds(i * half, half)
+        return remote(
+            dyn16.at[q, :, piece],
+            col16.at[dst_slot, :, piece],
+            bulk_s.at[q, i],
+            bulk_r.at[dst_slot, i],
+            (s, h, q),
+        )
+
+    def send_bulk(q, i):
         @pl.when(l != q)
         def _():
-            bulk_copy(q, l).start()
+            bulk_copy(q, l, i).start()
 
         @pl.when(l == q)
         def _():
-            col16[q] = dyn16[q]
+            piece = pl.ds(i * half, half)
+            col16[q, :, piece] = dyn16[q, :, piece]
 
     lo_c, hi_c = B - HALO, R - B + HALO
     k_mid = staged(kap_ref[lo_c:hi_c], steps)
@@ -259,9 +270,10 @@
         keep(v, 0, lo_c, g, [(q, q * B) for q in range(1, L - 1)])
         return 0
 
-    lax.fori_loop(0, G, middle, 0, unroll=5 if G % 5 == 0 else 1)
-    for q in range(1, L - 1):
-        send_bulk(q)
+    for i in range(parts):
+        lax.fori_loop(i * half, (i + 1) * half, middle, 0, unroll=5 if half % 5 == 0 else 1)
+        for q in range(1, L - 1):
+            send_bulk(q, i)
 
     for c in halos:
         c.wait_recv()
@@ -278,8 +290,9 @@
         keep(v, HALO, 0, g, [(0, 0)])
         return 0
 
-    lax.fori_loop(0, G, top, 0, unroll=5 if G % 5 == 0 else 1)
-    send_bulk(0)
+    for i in range(parts):
+        lax.fori_loop(i * half, (i + 1) * half, top, 0, unroll=5 if half % 5 == 0 else 1)
+        send_bulk(0, i)
 
     k_bot = staged(jnp.concatenate([kap_ref[R - B - HALO : R], halo_k[1]], axis=0), steps)
 
@@ -295,8 +308,9 @@
         keep(v, HALO, R - B, g, [(L - 1, R - B)])
         return 0
 
-    lax.fori_loop(0, G, bottom, 0, unroll=5 if G % 5 == 0 else 1)
-    send_bulk(L - 1)
+    for i in range(parts):
+        lax.fori_loop(i * half, (i + 1) * half, bottom, 0, unroll=5 if half % 5 == 0 else 1)
+        send_bulk(L - 1, i)
 
     for c in loads[3:8]:
         c.wait()
@@ -377,7 +391,8 @@
 
         @pl.when(l != q)
         def _(q=q):
-            bulk_copy(q, q).wait_recv()
+            for i in range(parts):
+                bulk_copy(q, q, i).wait_recv()
 
     def ret_copy(q, t, slot):
         return remote(y16.at[q, t], yr.at[slot, t], ret_s.at[q, t], ret_r.at[slot, t], (s, h, q))
@@ -428,7 +443,7 @@
                     )
             return 0
 
-        lax.fori_loop(0, G, finish, 0)
+        lax.fori_loop(0, G, finish, 0, unroll=5 if G % 5 == 0 else 1)
 
     for c in halos:
         c.wait_send()
@@ -441,7 +456,8 @@
 
         @pl.when(l != q)
         def _(q=q):
-            bulk_copy(q, l).wait_send()
+            for i in range(parts):
+                bulk_copy(q, l, i).wait_send()
             for t in range(T):
                 ret_copy(q, t, l).wait_send()
 
@@ -525,8 +541,8 @@
             dma,
             dma,
             dma,
-            dma((L,)),
-            dma((L,)),
+            dma((L, 2)),
+            dma((L, 2)),
             dma((L - 1,)),
             dma((L,)),
             dma((L, T)),

time: 32.4 us -> 31.4 us (0.969)
  Pallas kernels: 30.1 us -> 29 us
    pallas_call x1, Pallas kernels: 30.1 us -> 29 us  [per_device(): pl.pallas_call(functools.partial(kernel, (H, L, K, R, W)), out_shape=(plt...]
where the time goes in v4:
time: 31.4 us; the launch traced here: 31.2 us
  Pallas kernels  29 us (92%)
  local copies, waits for them, and re-layouts  1.55 us (5%)
  between operations  0.64 us (2%)
    pallas_call x1, Pallas kernels, per_device(): pl.pallas_call(functools.partial(kernel, (H, L, K, R, W)), out_shape=(plt...  29 us
    unnamed x2, local copies, waits for them, and re-layouts  1.55 us

profile of v4, /device:TPU:0, one launch (start us, length us, event | category | flops | bytes accessed | tf_op | source)
XLA Modules:
  0.0 31.2 jit_solution(14162285523450795278)
XLA Ops:
  0.6 29.0 %shard_map.104 = (f32[20,96,128]{2,1,0:T(8,128)S(1)}, f32[24,128]{1,0:T(8,128)S(1)}) custom-call(f32[20,96,128]{2,1,0:T(8,128)} %bitcast.11, f32[96,128]{1,0:T(8,128)} %bitcast.12, s32[24,128]{1,0:T(8,128)} %bitcast.14, s32[3,1,24]{2,1,0:T(1,128)} %bitcast.15, s32[1,24]{1,0:T(1,128)} %counts_hbm.1, bf16[9216,128]{1,0:T(8,128)(2,1)} %bitcast.10, ...), custom_call_target="tpu_custom_call" | custom-call | tf_op jit(solution)/shard_map/pallas_call | solution.py:503
  29.7 0.9 %copy.13 = f32[1,20,96,128]{3,2,1,0:T(8,128)} copy(f32[1,20,96,128]{3,2,1,0:T(8,128)S(1)} %bitcast.8) | data formatting | bytes 1966080
  30.6 0.6 %copy.14 = f32[1,24,128]{2,1,0:T(8,128)} copy(f32[1,24,128]{2,1,0:T(8,128)S(1)} %bitcast.9) | data formatting | bytes 24576

commit v5 on v4

--- a/solution.py
+++ b/solution.py
@@ -154,8 +154,6 @@
     def add_level(k, acc):
         return acc + exp_ref[0, l * K + k] * x_ref[k]
 
-    p_buf[...] = lax.fori_loop(0, K, add_level, jnp.zeros((R, W), F32), unroll=4)
-
     loads[2].wait()
     pl.semaphore_wait(barrier, (L - 1) + 2 + L + 2)
 
@@ -167,6 +165,8 @@
     ]
     for c in halos:
         c.start()
+
+    p_buf[...] = lax.fori_loop(0, K, add_level, jnp.zeros((R, W), F32), unroll=4)
 
     def window(q):
         lo = max(q * B - MARGIN, 0)

time: 31.4 us -> 31.4 us (level)
  no operation moved by 1% of the time
where the time goes in v5:
time: 31.4 us; the launch traced here: 31.2 us
  Pallas kernels  29 us (92%)
  local copies, waits for them, and re-layouts  1.55 us (5%)
  between operations  0.64 us (2%)
    pallas_call x1, Pallas kernels, per_device(): pl.pallas_call(functools.partial(kernel, (H, L, K, R, W)), out_shape=(plt...  29 us
    unnamed x2, local copies, waits for them, and re-layouts  1.55 us

profile of v5, /device:TPU:0, one launch (start us, length us, event | category | flops | bytes accessed | tf_op | source)
XLA Modules:
  0.0 31.2 jit_solution(14633108751623209791)
XLA Ops:
  0.6 29.0 %shard_map.104 = (f32[20,96,128]{2,1,0:T(8,128)S(1)}, f32[24,128]{1,0:T(8,128)S(1)}) custom-call(f32[20,96,128]{2,1,0:T(8,128)} %bitcast.11, f32[96,128]{1,0:T(8,128)} %bitcast.12, s32[24,128]{1,0:T(8,128)} %bitcast.14, s32[3,1,24]{2,1,0:T(1,128)} %bitcast.15, s32[1,24]{1,0:T(1,128)} %counts_hbm.1, bf16[9216,128]{1,0:T(8,128)(2,1)} %bitcast.10, ...), custom_call_target="tpu_custom_call" | custom-call | tf_op jit(solution)/shard_map/pallas_call | solution.py:503
  29.7 0.9 %copy.13 = f32[1,20,96,128]{3,2,1,0:T(8,128)} copy(f32[1,20,96,128]{3,2,1,0:T(8,128)S(1)} %bitcast.8) | data formatting | bytes 1966080
  30.6 0.6 %copy.14 = f32[1,24,128]{2,1,0:T(8,128)} copy(f32[1,24,128]{2,1,0:T(8,128)S(1)} %bitcast.9) | data formatting | bytes 24576
